TPU v7x, 32 devices: a whole 2x2x4 slice. The times are simulated.
32 devices in a mesh: wide: 16 (over z, y, core), narrow: 2 (over x).
Axes of the slice: x: 2, y: 2, z: 4, core: 2. Of those that a mesh axis runs over, the one named last changes fastest.
Arguments:
- tokens_short: bfloat16 [128, 128, 768], P(('wide', 'narrow')), may hold values from -6 to 6
- lengths_short: int32 [128], P(('wide', 'narrow')), may hold values from 20 to 128
- tokens_long: bfloat16 [128, 320, 768], P(('wide', 'narrow')), may hold values from -6 to 6
- lengths_long: int32 [128], P(('wide', 'narrow')), may hold values from 129 to 320
- query_weight: bfloat16 [768, 768], P(('wide', 'narrow')), may hold values from -0.3125 to 0.3125
- key_weight: bfloat16 [768, 768], P(('wide', 'narrow')), may hold values from -0.3125 to 0.3125
- value_weight: bfloat16 [768, 768], P(('wide', 'narrow')), may hold values from -0.21875 to 0.21875
- out_weight: bfloat16 [768, 768], P(('wide', 'narrow')), may hold values from -0.625 to 0.625
- up_weight: bfloat16 [768, 3072], P(('wide', 'narrow')), may hold values from -0.21875 to 0.21875
- down_weight: bfloat16 [3072, 768], P(('wide', 'narrow')), may hold values from -0.109375 to 0.109375
- embed_weight: bfloat16 [768, 128], P(('wide', 'narrow')), may hold values from -0.21875 to 0.21875
- query_bias: bfloat16 [768], P(('wide', 'narrow')), may hold values from -3 to 3
- value_bias: bfloat16 [768], P(('wide', 'narrow')), may hold values from -3 to 3
- out_bias: bfloat16 [768], P(('wide', 'narrow')), may hold values from -3 to 3
- attention_gain: bfloat16 [768], P(('wide', 'narrow')), may hold values from 0.5 to 1.5
- attention_shift: bfloat16 [768], P(('wide', 'narrow')), may hold values from -2 to 2
- up_bias: bfloat16 [3072], P(('wide', 'narrow')), may hold values from -3 to 3
- down_bias: bfloat16 [768], P(('wide', 'narrow')), may hold values from -3 to 3
- final_gain: bfloat16 [768], P(('wide', 'narrow')), may hold values from 0.5 to 1.5
- final_shift: bfloat16 [768], P(('wide', 'narrow')), may hold values from -2 to 2
- cotangent_short: bfloat16 [128, 128, 128], P(('wide', 'narrow')), may hold values from -6 to 6
- cotangent_long: bfloat16 [128, 320, 128], P(('wide', 'narrow')), may hold values from -6 to 6
Outputs:
- embed_short: float32 [128, 128, 128], P(('wide', 'narrow'))
- embed_long: float32 [128, 320, 128], P(('wide', 'narrow'))
- grad_tokens_short: float32 [128, 128, 768], P(('wide', 'narrow'))
- grad_tokens_long: float32 [128, 320, 768], P(('wide', 'narrow'))
- grad_query_weight: float32 [768, 768], P(('wide', 'narrow'))
- grad_key_weight: float32 [768, 768], P(('wide', 'narrow'))
- grad_value_weight: float32 [768, 768], P(('wide', 'narrow'))
- grad_out_weight: float32 [768, 768], P(('wide', 'narrow'))
- grad_up_weight: float32 [768, 3072], P(('wide', 'narrow'))
- grad_down_weight: float32 [3072, 768], P(('wide', 'narrow'))
- grad_embed_weight: float32 [768, 128], P(('wide', 'narrow'))
- grad_query_bias: float32 [768], P(('wide', 'narrow'))
- grad_value_bias: float32 [768], P(('wide', 'narrow'))
- grad_out_bias: float32 [768], P(('wide', 'narrow'))
- grad_attention_gain: float32 [768], P(('wide', 'narrow'))
- grad_attention_shift: float32 [768], P(('wide', 'narrow'))
- grad_up_bias: float32 [3072], P(('wide', 'narrow'))
- grad_down_bias: float32 [768], P(('wide', 'narrow'))
- grad_final_gain: float32 [768], P(('wide', 'narrow'))
- grad_final_shift: float32 [768], P(('wide', 'narrow'))
All inputs are finite; a program needn't handle non-finite values.
Results may differ from a plain program's by a relative error of at most 0.015.
The roundings to bfloat16 on the way count: a program that leaves them out, or rounds other values in their place, can miss the bound.
Values may be sent and summed in bfloat16 or wider, within the bound.
A program may use at most 256 MiB of HBM per device.

v0:
```python
import functools
import math

import jax
import jax.numpy as jnp
from jax import lax
from jax.experimental import pallas as pl
from jax.experimental.pallas import tpu as pltpu
from jax.sharding import PartitionSpec as P

MESH = pl.DeviceIdType.MESH

HD = 64
P_SIZE = 128


norm_epsilon = 1e-12
unit_epsilon = 1e-06
masked_fill = -1000000000.0


def layer_norm(residual, norm_gain, norm_shift):
    center = residual - jnp.mean(residual, axis=-1, keepdims=True)
    variance = jnp.mean(center * center, axis=-1, keepdims=True)
    return center * lax.rsqrt(variance + norm_epsilon) * norm_gain + norm_shift


def gelu_exact(pre_act):
    return 0.5 * pre_act * (1.0 + lax.erf(pre_act * (1.0 / math.sqrt(2.0))))


def normalize(embedding, token_mask):
    squares = jnp.sum(embedding * embedding, axis=-1, keepdims=True)
    return math.sqrt(P_SIZE) * embedding * lax.rsqrt(squares + unit_epsilon) * token_mask[..., None]


def soft_weights(scaled, key_mask):
    masked = jnp.where(key_mask, scaled, masked_fill)
    row_peak = jnp.max(masked, axis=-1, keepdims=True)
    exponent = jnp.exp(masked - row_peak)
    return exponent / jnp.sum(exponent, axis=-1, keepdims=True)


def matmul(left_side, right_side, form):
    return jnp.einsum(form, left_side, right_side, preferred_element_type=jnp.float32)


def forward(tokens, lengths, full_weights):
    (
        query_weight,
        key_weight,
        value_weight,
        out_weight,
        up_weight,
        down_weight,
        embed_weight,
        query_bias,
        value_bias,
        out_bias,
        attention_gain,
        attention_shift,
        up_bias,
        down_bias,
        final_gain,
        final_shift,
    ) = full_weights
    seq_count, length, model_width = tokens.shape
    head_count = model_width // HD
    score_scale = 1.0 / math.sqrt(HD)
    positions = jnp.arange(length, dtype=jnp.int32)
    token_mask = (positions[None, :] < lengths[:, None]).astype(jnp.float32)
    key_mask = token_mask[:, None, None, :] > 0.5
    query_low = (matmul(tokens, query_weight, "bld,de->ble") + query_bias).astype(jnp.bfloat16)
    query_low = query_low.reshape(seq_count, length, head_count, HD)
    key_low = matmul(tokens, key_weight, "bld,de->ble").astype(jnp.bfloat16)
    key_low = key_low.reshape(seq_count, length, head_count, HD)
    value_low = (matmul(tokens, value_weight, "bld,de->ble") + value_bias).astype(jnp.bfloat16)
    value_low = value_low.reshape(seq_count, length, head_count, HD)
    raw_scores = matmul(query_low, key_low, "bqhe,bkhe->bhqk") * score_scale
    attn_probs = soft_weights(raw_scores, key_mask)
    probs_low = attn_probs.astype(jnp.bfloat16)
    context_low = matmul(probs_low, value_low, "bhqk,bkhe->bqhe")
    context_low = context_low.reshape(seq_count, length, model_width).astype(jnp.bfloat16)
    attn_out = matmul(context_low, out_weight, "bld,de->ble") + out_bias
    resid_one = tokens.astype(jnp.float32) + attn_out
    normed_one = layer_norm(resid_one, attention_gain, attention_shift)
    hidden_low = normed_one.astype(jnp.bfloat16)
    pre_act = matmul(hidden_low, up_weight, "bld,df->blf") + up_bias
    act_low = gelu_exact(pre_act).astype(jnp.bfloat16)
    ffn_out = matmul(act_low, down_weight, "blf,fd->bld") + down_bias
    resid_two = normed_one + ffn_out
    final_low = layer_norm(resid_two, final_gain, final_shift).astype(jnp.bfloat16)
    embedding = matmul(final_low, embed_weight, "bld,dp->blp")
    result = normalize(embedding, token_mask)
    saved = (
        tokens,
        token_mask,
        query_low,
        key_low,
        value_low,
        attn_probs,
        probs_low,
        context_low,
        resid_one,
        hidden_low,
        pre_act,
        act_low,
        resid_two,
        final_low,
        embedding,
    )
    return (result, saved)


def backward(saved, full_weights, cotangent):
    (
        tokens,
        token_mask,
        query_low,
        key_low,
        value_low,
        attn_probs,
        probs_low,
        context_low,
        resid_one,
        hidden_low,
        pre_act,
        act_low,
        resid_two,
        final_low,
        embedding,
    ) = saved
    (
        query_weight,
        key_weight,
        value_weight,
        out_weight,
        up_weight,
        down_weight,
        embed_weight,
        query_bias,
        value_bias,
        out_bias,
        attention_gain,
        attention_shift,
        up_bias,
        down_bias,
        final_gain,
        final_shift,
    ) = full_weights
    seq_count, length, model_width = tokens.shape
    score_scale = 1.0 / math.sqrt(HD)
    _, pull_norm = jax.vjp(lambda vector: normalize(vector, token_mask), embedding)
    (embed_grad,) = pull_norm(cotangent.astype(jnp.float32))
    embed_low = embed_grad.astype(jnp.bfloat16)
    grad_embed = matmul(final_low, embed_low, "bld,blp->dp")
    final_grad = matmul(embed_low, embed_weight, "blp,dp->bld")
    _, pull_two = jax.vjp(
        layer_norm, resid_two, final_gain.astype(jnp.float32), final_shift.astype(jnp.float32)
    )
    resid_two_grad, grad_final_gain, grad_final_shift = pull_two(final_grad)
    ffn_low = resid_two_grad.astype(jnp.bfloat16)
    grad_down_bias = jnp.sum(ffn_low, axis=(0, 1), dtype=jnp.float32)
    grad_down = matmul(act_low, ffn_low, "blf,bld->fd")
    act_grad = matmul(ffn_low, down_weight, "bld,fd->blf")
    _, pull_gelu = jax.vjp(gelu_exact, pre_act)
    (pre_grad,) = pull_gelu(act_grad)
    pre_low = pre_grad.astype(jnp.bfloat16)
    grad_up_bias = jnp.sum(pre_low, axis=(0, 1), dtype=jnp.float32)
    grad_up = matmul(hidden_low, pre_low, "bld,blf->df")
    normed_grad = resid_two_grad + matmul(pre_low, up_weight, "blf,df->bld")
    _, pull_one = jax.vjp(
        layer_norm,
        resid_one,
        attention_gain.astype(jnp.float32),
        attention_shift.astype(jnp.float32),
    )
    resid_one_grad, grad_attention_gain, grad_attention_shift = pull_one(normed_grad)
    attn_low = resid_one_grad.astype(jnp.bfloat16)
    grad_out_bias = jnp.sum(attn_low, axis=(0, 1), dtype=jnp.float32)
    grad_out = matmul(context_low, attn_low, "bld,ble->de")
    context_grad = matmul(attn_low, out_weight, "ble,de->bld").astype(jnp.bfloat16)
    context_grad = context_grad.reshape(seq_count, length, -1, HD)
    value_grad = matmul(probs_low, context_grad, "bhqk,bqhe->bkhe")
    probs_grad = matmul(context_grad, value_low, "bqhe,bkhe->bhqk")
    score_low = attn_probs * (probs_grad - jnp.sum(probs_grad * attn_probs, axis=-1, keepdims=True))
    score_low = score_low.astype(jnp.bfloat16)
    query_grad = (matmul(score_low, key_low, "bhqk,bkhe->bqhe") * score_scale).astype(jnp.bfloat16)
    query_grad = query_grad.reshape(seq_count, length, model_width)
    key_grad = (matmul(score_low, query_low, "bhqk,bqhe->bkhe") * score_scale).astype(jnp.bfloat16)
    key_grad = key_grad.reshape(seq_count, length, model_width)
    value_grad_low = value_grad.astype(jnp.bfloat16).reshape(seq_count, length, model_width)
    grad_query_bias = jnp.sum(query_grad, axis=(0, 1), dtype=jnp.float32)
    grad_value_bias = jnp.sum(value_grad_low, axis=(0, 1), dtype=jnp.float32)
    grad_query = matmul(tokens, query_grad, "bld,ble->de")
    grad_key = matmul(tokens, key_grad, "bld,ble->de")
    grad_value = matmul(tokens, value_grad_low, "bld,ble->de")
    input_grad = (
        resid_one_grad
        + matmul(query_grad, query_weight, "ble,de->bld")
        + matmul(key_grad, key_weight, "ble,de->bld")
        + matmul(value_grad_low, value_weight, "ble,de->bld")
    )
    gradients = (
        grad_query,
        grad_key,
        grad_value,
        grad_out,
        grad_up,
        grad_down,
        grad_embed,
        grad_query_bias,
        grad_value_bias,
        grad_out_bias,
        grad_attention_gain,
        grad_attention_shift,
        grad_up_bias,
        grad_down_bias,
        grad_final_gain,
        grad_final_shift,
    )
    return (input_grad, gradients)


BOTH = ("wide", "narrow")
WIRE = ((48, 512), (48, 768), (48, 512), (48, 1536), (96, 768))
CUT = (256, 384, 256, 768, 384)
ROWS = 1792
SHORT = 512
COPIES = 39


def place():
    wide = lax.axis_index("wide")
    return wide // 4, (wide // 2) % 2, wide % 2, lax.axis_index("narrow")


def greet(z, y, c, x):
    partners = [device((z + d) % 4, y, c, x) for d in (1, 2, 3)]
    partners += [device(z, 1 - y, c, x), device(z, y, 1 - c, x), device(z, y, c, 1 - x)]
    barrier = pltpu.get_barrier_semaphore()
    for partner in partners:
        pl.semaphore_signal(barrier, inc=1, device_id=partner, device_id_type=MESH)
    pl.semaphore_wait(barrier, len(partners))


def device(z, y, c, x):
    return (z * 4 + y * 2 + c, x)


class Lazy:
    def __init__(self, make):
        self.make = make

    def __getitem__(self, way):
        return self.make(way)


class Gather:
    def __init__(self, held, cut, send, recv, first):
        self.held, self.cut, self.send, self.recv, self.first = held, cut, send, recv, first
        self.z, self.y, self.c, self.x = place()

    def view(self, block, half):
        if half is None:
            return self.held.at[block]
        lanes = self.held.shape[-1]
        low, size = ((0, self.cut), (self.cut, lanes - self.cut))[half]
        return self.held.at[(*block, slice(None), pl.ds(low, size))]

    def plan(self, slot, out, into, half, target):
        def copy(block):
            return pltpu.make_async_remote_copy(
                src_ref=self.view(block, half),
                dst_ref=self.view(block, half),
                send_sem=self.send.at[self.first + slot],
                recv_sem=self.recv.at[self.first + slot],
                device_id=target,
                device_id_type=MESH,
            )

        return Lazy(lambda way: copy((out, into)[way]))

    def along_z(self, d):
        z, y, c, x = self.z, self.y, self.c, self.x
        return self.plan(d - 1, (z, y, c, x), ((z + 4 - d) % 4, y, c, x), None, device((z + d) % 4, y, c, x))

    def to_x(self, d):
        z, y, c, x = (self.z + 4 - d) % 4, self.y, self.c, self.x
        return self.plan(3 + d, (z, y, c, x), (z, y, c, 1 - x), None, device(self.z, y, c, 1 - x))

    def to_y(self, d):
        z, y, c, x = (self.z + 4 - d) % 4, self.y, self.c, self.x
        return self.plan(7 + d, (z, y, c, x), (z, 1 - y, c, x), None, device(self.z, 1 - y, c, x))

    def corner(self, d, half):
        z, y, c, x = (self.z + 4 - d) % 4, self.y, self.c, self.x
        if half == 0:
            return self.plan(11 + d, (z, y, c, 1 - x), (z, 1 - y, c, 1 - x), 0, device(self.z, 1 - y, c, x))
        return self.plan(15 + d, (z, 1 - y, c, x), (z, 1 - y, c, 1 - x), 1, device(self.z, y, c, 1 - x))

    def to_core(self, d, kind):
        z, c = (self.z + 4 - d) % 4, self.c
        y = 1 - self.y if kind >= 2 else self.y
        x = 1 - self.x if kind in (1, 3, 4) else self.x
        half = kind - 3 if kind >= 3 else None
        return self.plan(19 + 4 * kind + d, (z, y, c, x), (z, y, 1 - c, x), half, device(self.z, self.y, 1 - c, self.x))

    def start_z(self):
        for d in (1, 2, 3):
            self.along_z(d)[0].start()

    def spread(self, d):
        self.to_x(d)[0].start()
        self.to_y(d)[0].start()
        self.to_core(d, 0)[0].start()

    def column(self, d):
        self.along_z(d)[1].wait_recv()
        self.spread(d)

    def turn(self, d):
        self.to_x(d)[1].wait_recv()
        self.corner(d, 0)[0].start()
        self.to_core(d, 1)[0].start()
        self.to_y(d)[1].wait_recv()
        self.corner(d, 1)[0].start()
        self.to_core(d, 2)[0].start()

    def finish(self, d):
        for half in (0, 1):
            self.corner(d, half)[1].wait_recv()
            self.to_core(d, 3 + half)[0].start()

    def arrive(self):
        for d in range(4):
            for kind in range(5):
                self.to_core(d, kind)[1].wait_recv()

    def drain(self):
        for d in range(4):
            if d:
                self.along_z(d)[0].wait_send()
            self.to_x(d)[0].wait_send()
            self.to_y(d)[0].wait_send()
            for half in (0, 1):
                self.corner(d, half)[0].wait_send()
            for kind in range(5):
                self.to_core(d, kind)[0].wait_send()


def stack_halves(whole):
    half = whole.shape[1] // 2
    return jnp.concatenate([whole[:, :half], whole[:, half:]], axis=0).astype(jnp.bfloat16)


def unpack_rows(held, targets):
    def pair(p, carry):
        z, y, c = p // 4, (p // 2) % 2, p % 2
        one, two = held[z, y, c, 0].astype(jnp.float32), held[z, y, c, 1].astype(jnp.float32)
        for side, low, ref, column, lanes in targets:
            rows = slice(24 * side, 24 * side + 24)
            both = jnp.concatenate([one[rows, low : low + lanes], two[rows, low : low + lanes]], axis=0)
            ref[pl.ds(pl.multiple_of(p * 48, 48), 48), column : column + lanes] = both.astype(jnp.bfloat16)
        return carry

    lax.fori_loop(0, 16, pair, 0)


NN = (((1,), (0,)), ((), ()))
NT = (((1,), (1,)), ((), ()))
TN = (((0,), (0,)), ((), ()))


def dot(left, right, dims):
    return lax.dot_general(left, right, dims, preferred_element_type=jnp.float32)


def padded(length):
    return -(-length // 128) * 128


def two_heads(pair, width):
    length = pair.shape[0]
    lane = lax.broadcasted_iota(jnp.int32, (length, 128), 1)
    parts = []
    for here in (lane < 64, lane >= 64):
        parts.append(jnp.where(here, pair, jnp.bfloat16(0)))
        if width > length:
            parts.append(jnp.zeros((width - length, 128), jnp.bfloat16))
    return jnp.concatenate(parts, axis=0)


def attend(qkv, context, probs, row, length, valid, first, last):
    rows = pl.ds(row, length)
    width = padded(length)
    fill = jnp.where(lax.broadcasted_iota(jnp.int32, (1, width), 1) < valid, 0.0, masked_fill)

    def pair(p):
        at = lambda base: pl.ds(base + p * 128, 128)
        query = qkv[rows, at(0)] * jnp.bfloat16(1.0 / math.sqrt(HD))
        key, value = qkv[rows, at(768)], qkv[rows, at(1536)]
        scores = dot(query, two_heads(key, width), NT)
        parts = []
        for h in (0, 1):
            masked = scores[:, width * h : width * h + width] + fill
            exponent = jnp.exp(masked - jnp.max(masked, axis=1, keepdims=True))
            scale = 1.0 / jnp.sum(exponent, axis=1, keepdims=True)
            parts.append((exponent * scale).astype(jnp.bfloat16))
        low = jnp.concatenate(parts, axis=1)
        probs[p] = low
        context[rows, at(0)] = dot(low, two_heads(value, width), NN).astype(jnp.bfloat16)

    for p in range(first, last):
        pair(p)


def spread_table(group, lanes):
    lane = lax.broadcasted_iota(jnp.int32, (128, lanes), 1).astype(jnp.float32)
    row = lax.broadcasted_iota(jnp.int32, (128, lanes), 0).astype(jnp.float32)
    return (lane - group * jnp.floor((lane + 0.5) * (1.0 / group)) == row).astype(jnp.bfloat16)


def natural_vectors(held, vec_out):
    blocks = [held[p // 8, (p // 4) % 2, (p // 2) % 2, p % 2, :16, 384:512] for p in range(32)]
    stacked = jnp.concatenate(blocks, axis=0)
    wide = dot(stacked, spread_table(24, 768), NN)
    lane = lax.broadcasted_iota(jnp.int32, (512, 768), 1)
    start = (lax.broadcasted_iota(jnp.int32, (512, 768), 0) >> 4) * 24
    wide = jnp.where((lane >= start) & (lane < start + 24), wide, 0.0)
    vec_out[:, :768] = jnp.sum(wide.reshape(32, 16, 768), axis=0)
    picked = dot(
        (lax.broadcasted_iota(jnp.int32, (32, 512), 1) == lax.broadcasted_iota(jnp.int32, (32, 512), 0) * 16 + 5).astype(jnp.bfloat16),
        stacked,
        NN,
    ).astype(jnp.bfloat16)
    wide = dot(picked, spread_table(96, 3072), NN)
    lane = lax.broadcasted_iota(jnp.int32, (32, 3072), 1)
    start = lax.broadcasted_iota(jnp.int32, (32, 3072), 0) * 96
    wide = jnp.where((lane >= start) & (lane < start + 96), wide, 0.0)
    vec_out[9:10, :] = jnp.sum(wide, axis=0, keepdims=True)


def first_kernel(
    len_short, len_long, xs, xl, cs, cl, q_ref, k_ref, v_ref, o_ref, u_ref, d_ref, e_ref, *rest
):
    vec_refs, rest = rest[:9], rest[9:]
    (qkv_out, out_out, up_out, embed_out, down_out, vec_out, proj_out, context_out, ps_out, pl_out, x_out, c_out), rest = rest[:12], rest[12:]
    h0, h1, h2, h3, h4, w_qkv, w_out, w_up, w_embed, proj, context, ps, pls, rows, send, recv, away = rest
    z, y, c, x = place()
    rows[...] = jnp.zeros_like(rows)
    for i, ref in enumerate(vec_refs):
        width = ref.shape[0]
        rows[i : i + 1, :width] = ref[...].astype(jnp.float32).reshape(1, width)
    wide = lambda ref: ref[...].astype(jnp.float32)
    h0[z, y, c, x, :, :384] = stack_halves(wide(q_ref))
    h0[z, y, c, x, :, 384:] = rows[...].astype(jnp.bfloat16)
    h1[z, y, c, x, :, :384] = stack_halves(wide(k_ref))
    h1[z, y, c, x, :, 384:] = stack_halves(wide(v_ref))
    h2[z, y, c, x, :, :384] = stack_halves(wide(o_ref))
    h2[z, y, c, x, :, 384:] = jnp.concatenate([wide(e_ref), wide(e_ref)], axis=0).astype(jnp.bfloat16)
    h3[z, y, c, x] = stack_halves(wide(u_ref))
    h4[z, y, c, x] = d_ref[...]
    greet(z, y, c, x)
    one, two, three, four, five = gathers = [Gather(h, CUT[i], send, recv, COPIES * i) for i, h in enumerate((h0, h1, h2, h3, h4))]
    for piece in gathers:
        piece.start_z()
    for piece in gathers:
        piece.spread(0)
    kept = []

    def keep(source, target):
        copy = pltpu.make_async_copy(source, target, away.at[len(kept)])
        copy.start()
        kept.append(copy)

    for source, target, low in ((xs, x_out, 0), (xl, x_out, SHORT), (cs, c_out, 0), (cl, c_out, SHORT)):
        keep(source, target.at[pl.ds(low, source.shape[0])])
    for d in (1, 2, 3):
        one.column(d)
    for d in (1, 2, 3):
        two.column(d)
    for d in range(4):
        one.turn(d)
    for d in (1, 2, 3):
        three.column(d)
    for d in range(4):
        two.turn(d)
    for d in range(4):
        one.finish(d)
    for d in (1, 2, 3):
        four.column(d)
    one.arrive()
    unpack_rows(h0, [(0, 0, w_qkv, 0, 384), (1, 0, w_qkv, 384, 384)])
    natural_vectors(h0, vec_out)
    for d in range(4):
        two.finish(d)
    step = lambda name, piece, *ds: [functools.partial(getattr(piece, name), d) for d in ds]
    hooks = iter([
        step("turn", three, 0, 1) + step("turn", four, 0) + step("turn", five, 0),
        step("turn", three, 2, 3) + step("turn", four, 1), step("finish", three, 0, 1) + step("column", five, 1),
        step("column", five, 2), step("column", five, 3), step("turn", four, 2), step("turn", four, 3),
        step("finish", three, 2, 3), step("finish", four, 0, 1), step("turn", five, 1), step("turn", five, 2),
        step("turn", five, 3), step("finish", four, 2, 3), step("finish", five, 0), step("finish", five, 1),
    ])

    def hook():
        for one_step in next(hooks):
            one_step()

    tiles = [(0, xs[...])] + [(SHORT + 320 * s, xl[320 * s : 320 * s + 320]) for s in range(4)]
    for part in range(3):
        if part == 1:
            two.arrive()
            unpack_rows(h1, [(0, 0, w_qkv, 768, 384), (1, 0, w_qkv, 1152, 384), (0, 384, w_qkv, 1536, 384), (1, 384, w_qkv, 1920, 384)])
            keep(w_qkv, qkv_out)
        lanes = slice(768 * part, 768 * part + 768)
        for row, tokens in tiles:
            result = dot(tokens, w_qkv[:, lanes], NN)
            if part != 1:
                result = result + vec_out[part // 2 : part // 2 + 1, :768]
            proj[row : row + tokens.shape[0], lanes] = result.astype(jnp.bfloat16)
        hook()
    keep(proj, proj_out)
    for s in range(4):
        attend(proj, context, ps.at[s], 128 * s, 128, len_short[s], 0, 6)
        hook()
    keep(ps, ps_out)
    slots = []
    for s in range(4):
        if s >= 2:
            slots[s - 2].wait()
        for part in (0, 3):
            attend(proj, context, pls.at[s % 2], SHORT + 320 * s, 320, len_long[s], part, part + 3)
            hook()
        copy = pltpu.make_async_copy(pls.at[s % 2], pl_out.at[s], away.at[12 + s])
        copy.start()
        slots.append(copy)
        if s == 1:
            three.arrive()
            unpack_rows(h2, [(0, 0, w_out, 0, 384), (1, 0, w_out, 384, 384), (0, 384, w_embed, 0, 128)])
            keep(w_out, out_out)
            keep(w_embed, embed_out)
    keep(context, context_out)
    four.arrive()
    unpack_rows(h3, [(0, 0, w_up, 0, 1536), (1, 0, w_up, 1536, 1536)])
    keep(w_up, up_out)
    for d in (2, 3):
        five.finish(d)
    five.arrive()
    keep(h4, down_out)
    for copy in kept + slots[2:]:
        copy.wait()
    for piece in gathers:
        piece.drain()


def first(len_short, len_long, xs, xl, cs, cl, shards):
    vmem, smem, anywhere = (pl.BlockSpec(memory_space=m) for m in (pltpu.VMEM, pltpu.SMEM, pl.ANY))
    low = lambda *dims: jax.ShapeDtypeStruct(dims, jnp.bfloat16)
    held = lambda *dims: pltpu.VMEM(dims, jnp.bfloat16)
    semaphores = lambda count: pltpu.SemaphoreType.DMA((count,))
    weights = [(768, 2304), (768, 768), (768, 3072), (768, 128)]
    return pl.pallas_call(
        first_kernel,
        out_shape=(
            *[low(*dims) for dims in weights], low(4, 2, 2, 2, *WIRE[4]),
            jax.ShapeDtypeStruct((16, 3072), jnp.float32),
            low(ROWS, 2304), low(ROWS, 768), low(4, 6, 128, 256), low(4, 6, 320, 768), low(ROWS, 768), low(ROWS, P_SIZE),
        ),
        in_specs=[smem] * 2 + [vmem] * 2 + [anywhere] * 2 + [vmem] * 16,
        out_specs=(anywhere,) * 5 + (vmem,) + (anywhere,) * 6,
        scratch_shapes=[held(4, 2, 2, 2, *dims) for dims in WIRE]
        + [held(*dims) for dims in weights]
        + [held(ROWS, 2304), held(ROWS, 768), held(4, 6, 128, 256), held(2, 6, 320, 768), pltpu.VMEM((48, 128), jnp.float32)]
        + [semaphores(COPIES * 5), semaphores(COPIES * 5), semaphores(16)],
        compiler_params=pltpu.CompilerParams(collective_id=0, has_side_effects=True, vmem_limit_bytes=62 * 2**20),
    )(len_short, len_long, xs, xl, cs, cl, *shards)


TILE = 448
PART = 224


def center(value):
    return value - jnp.mean(value, axis=1, keepdims=True)


def normal(value):
    value = center(value)
    scale = lax.rsqrt(jnp.mean(value * value, axis=1, keepdims=True) + norm_epsilon)
    return value * scale, scale


def normal_back(grad, unit, scale):
    inner = jnp.mean(grad * unit, axis=1, keepdims=True)
    return scale * (center(grad) - unit * inner)


def embed_copies(step, embedded, es_out, el_out, away):
    low, high = TILE * step, TILE * step + TILE
    cut = min(max(SHORT, low), high)
    copies = []
    if low < cut:
        copies.append((embedded.at[pl.ds(0, cut - low)], es_out.at[pl.ds(low, cut - low)]))
    if cut < high:
        copies.append((embedded.at[pl.ds(cut - low, high - cut)], el_out.at[pl.ds(cut - SHORT, high - cut)]))
    return [pltpu.make_async_copy(source, target, away.at[i]) for i, (source, target) in enumerate(copies)]


def token_kernel(
    len_short, len_long, x_ref, cot_ref, ctx_ref, w_out, w_up, w_down, w_embed, vec,
    es_out, el_out, act_out, pre_out, hidden_out, ffn_out, attn_out, final_out, eg_out, resid_out, cg_out, sums,
    slope, embedded, away,
):
    tile = pl.program_id(0)
    row = lambda k: vec[k : k + 1, :768]
    low = lambda value: value.astype(jnp.bfloat16)
    wide = lambda value: value.astype(jnp.float32)

    @pl.when(tile == 0)
    def _():
        sums[...] = jnp.zeros_like(sums)

    def add(k, value):
        sums[k : k + 1, : value.shape[1]] += jnp.sum(value, axis=0, keepdims=True)

    def chain(start):
        rows = slice(start, start + PART)
        mixed = wide(x_ref[rows]) + (dot(ctx_ref[rows], w_out[...], NN) + row(2))
        yield
        unit_one, scale_one = normal(mixed)
        normed_one = unit_one * row(3) + row(4)
        hidden = low(normed_one)
        hidden_out[rows] = hidden
        ffn = None
        for f in range(4):
            lanes = slice(768 * f, 768 * f + 768)
            pre = dot(hidden, w_up[:, lanes], NN) + vec[9:10, lanes]
            cdf = 0.5 + 0.5 * lax.erf(pre * (1.0 / math.sqrt(2.0)))
            act = low(pre * cdf)
            act_out[rows, lanes] = act
            slope[rows, lanes] = cdf + pre * (jnp.exp(-0.5 * pre * pre) * (1.0 / math.sqrt(2.0 * math.pi)))
            part = dot(act, w_down[lanes, :], NN)
            ffn = part if ffn is None else ffn + part
        yield
        unit_two, scale_two = normal(normed_one + (ffn + row(6)))
        final = low(unit_two * row(7) + row(8))
        final_out[rows] = final
        embedding = dot(final, w_embed[...], NN)
        inverse = lax.rsqrt(jnp.sum(embedding * embedding, axis=1, keepdims=True) + unit_epsilon)
        at = lax.broadcasted_iota(jnp.int32, (PART, 1), 0) + (tile * TILE + start)
        mask = jnp.zeros((PART, 1), jnp.float32)
        for sizes, low_row, stride in ((len_short, 0, 128), (len_long, SHORT, 320)):
            for s in range(4):
                begin = low_row + s * stride
                mask = mask + jnp.where((at >= begin) & (at < begin + sizes[s]), 1.0, 0.0)
        embedded[rows] = math.sqrt(P_SIZE) * embedding * inverse * mask
        grad = wide(cot_ref[rows]) * mask
        inner = jnp.sum(grad * embedding, axis=1, keepdims=True)
        embed_grad = low(math.sqrt(P_SIZE) * inverse * (grad - inverse * inverse * embedding * inner))
        eg_out[rows] = embed_grad
        final_grad = dot(embed_grad, w_embed[...], NT)
        yield
        add(7, final_grad * unit_two)
        add(8, final_grad)
        resid_two = normal_back(final_grad * row(7), unit_two, scale_two)
        ffn_grad = low(resid_two)
        ffn_out[rows] = ffn_grad
        add(6, wide(ffn_grad))
        normed_grad = resid_two
        for f in range(4):
            lanes = slice(768 * f, 768 * f + 768)
            pre_grad = low(dot(ffn_grad, w_down[lanes, :], NT) * slope[rows, lanes])
            pre_out[rows, lanes] = pre_grad
            sums[9:10, lanes] += jnp.sum(wide(pre_grad), axis=0, keepdims=True)
            normed_grad = normed_grad + dot(pre_grad, w_up[:, lanes], NT)
        yield
        add(3, normed_grad * unit_one)
        add(4, normed_grad)
        resid_one = normal_back(normed_grad * row(3), unit_one, scale_one)
        resid_out[rows] = resid_one
        attn_grad = low(resid_one)
        attn_out[rows] = attn_grad
        add(2, wide(attn_grad))
        cg_out[rows] = low(dot(attn_grad, w_out[...], NT))
        yield

    chains = [chain(start) for start in range(0, TILE, PART)]
    for _ in range(5):
        for one in chains:
            next(one)

    def embeds(act):
        for step in range(ROWS // TILE):

            @pl.when(tile == step)
            def _():
                for copy in embed_copies(step, embedded, es_out, el_out, away):
                    getattr(copy, act)()

    embeds("start")
    embeds("wait")


def token_chain(len_short, len_long, x, cot, context, w_out, w_up, w_down, w_embed, vec):
    smem, anywhere = pl.BlockSpec(memory_space=pltpu.SMEM), pl.BlockSpec(memory_space=pl.ANY)
    every = lambda lanes: pl.BlockSpec((TILE, lanes), lambda i: (i, 0))
    whole = lambda array: pl.BlockSpec(array.shape, lambda i: (0, 0), pipeline_mode=pl.Buffered(1))
    shape = lambda kind, *dims: jax.ShapeDtypeStruct(dims, kind)
    low = lambda lanes: shape(jnp.bfloat16, ROWS, lanes)
    return pl.pallas_call(
        token_kernel,
        grid=(ROWS // TILE,),
        out_shape=(
            shape(jnp.float32, SHORT, P_SIZE), shape(jnp.float32, ROWS - SHORT, P_SIZE),
            low(3072), low(3072), low(768), low(768), low(768), low(768), low(P_SIZE),
            shape(jnp.float32, ROWS, 768), low(768), shape(jnp.float32, 16, 3072),
        ),
        in_specs=[smem, smem, every(768), every(P_SIZE), every(768)] + [whole(one) for one in (w_out, w_up, w_down, w_embed, vec)],
        out_specs=(
            anywhere, anywhere, every(3072), every(3072), every(768), every(768), every(768), every(768), every(P_SIZE),
            every(768), every(768), pl.BlockSpec((16, 3072), lambda i: (0, 0)),
        ),
        scratch_shapes=[pltpu.VMEM((TILE, 3072), jnp.float32), pltpu.VMEM((TILE, P_SIZE), jnp.float32), pltpu.SemaphoreType.DMA((2,))],
        compiler_params=pltpu.CompilerParams(vmem_limit_bytes=62 * 2**20),
    )(len_short, len_long, x, cot, context, w_out, w_up, w_down, w_embed, vec)


class Scatter:
    def __init__(self, mine, cut, work, send, recv, local, number):
        self.mine, self.cut, self.send, self.recv, self.first = mine, cut, send, recv, SUMS * number
        self.core_in, self.total, self.corner_y, self.corner_x, self.from_x, self.from_y, self.from_z = work
        self.z, self.y, self.c, self.x = place()
        self.own = pltpu.make_async_copy(mine.at[:, :, self.c], self.total, local.at[number])

    def copy(self, slot, source, target, partner):
        return pltpu.make_async_remote_copy(
            src_ref=source,
            dst_ref=target,
            send_sem=self.send.at[self.first + slot],
            recv_sem=self.recv.at[self.first + slot],
            device_id=partner,
            device_id_type=MESH,
        )

    def spot(self, kind):
        return (1 - self.y if kind in (0, 2) else self.y), (1 - self.x if kind in (0, 1) else self.x)

    def core(self, kind):
        y, x = self.spot(kind)
        return self.copy(
            kind,
            self.mine.at[:, y, 1 - self.c, x],
            self.core_in.at[:, y, x],
            device(self.z, self.y, 1 - self.c, self.x),
        )

    def corner(self, d, half):
        z = (self.z + d) % 4
        y, x = self.spot(0)
        low, size = ((0, self.cut), (self.cut, self.total.shape[-1] - self.cut))[half]
        source = self.total.at[z, y, x, :, pl.ds(low, size)]
        if half == 0:
            return self.copy(4 + d, source, self.corner_y.at[z], device(self.z, 1 - self.y, self.c, self.x))
        return self.copy(8 + d, source, self.corner_x.at[z], device(self.z, self.y, self.c, 1 - self.x))

    def to_x(self, d):
        z = (self.z + d) % 4
        return self.copy(12 + d, self.total.at[z, self.y, 1 - self.x], self.from_x.at[z], device(self.z, self.y, self.c, 1 - self.x))

    def to_y(self, d):
        z = (self.z + d) % 4
        return self.copy(16 + d, self.total.at[z, 1 - self.y, self.x], self.from_y.at[z], device(self.z, 1 - self.y, self.c, self.x))

    def along_z(self, d):
        z = (self.z + d) % 4
        return self.copy(19 + d, self.total.at[z, self.y, self.x], self.from_z.at[d - 1], device(z, self.y, self.c, self.x))

    def start(self):
        self.own.start()
        for kind in range(4):
            self.core(kind).start()

    def merge(self, kind):
        if kind == 0:
            self.own.wait()
        self.core(kind).wait_recv()
        y, x = self.spot(kind)

        def add(z, carry):
            self.total[z, y, x] = self.total[z, y, x] + self.core_in[z, y, x]
            return carry

        lax.fori_loop(0, 4, add, 0)
        if kind == 0:
            for d in (1, 2, 3, 0):
                self.corner(d, 0).start()
                self.corner(d, 1).start()

    def bend(self, d):
        z = (self.z + d) % 4
        self.corner(d, 0).wait_recv()
        self.total[z, self.y, 1 - self.x, :, : self.cut] = self.total[z, self.y, 1 - self.x, :, : self.cut] + self.corner_y[z]
        self.to_x(d).start()
        self.corner(d, 1).wait_recv()
        self.total[z, 1 - self.y, self.x, :, self.cut :] = self.total[z, 1 - self.y, self.x, :, self.cut :] + self.corner_x[z]
        self.to_y(d).start()

    def close(self, d):
        z = (self.z + d) % 4
        self.to_x(d).wait_recv()
        self.to_y(d).wait_recv()
        here = self.total[z, self.y, self.x].astype(jnp.float32) + self.from_x[z].astype(jnp.float32)
        self.total[z, self.y, self.x] = (here + self.from_y[z].astype(jnp.float32)).astype(jnp.bfloat16)
        if d:
            self.along_z(d).start()

    def result(self, store):
        total = self.total[self.z, self.y, self.x].astype(jnp.float32)
        for d in (1, 2, 3):
            self.along_z(d).wait_recv()
            total = total + self.from_z[d - 1].astype(jnp.float32)
        store[...] = total

    def drain(self):
        for kind in range(4):
            self.core(kind).wait_send()
        for d in range(4):
            self.corner(d, 0).wait_send()
            self.corner(d, 1).wait_send()
            self.to_x(d).wait_send()
            self.to_y(d).wait_send()
            if d:
                self.along_z(d).wait_send()


SUMS = 23
BACK = ((96, 768), (48, 1536), (48, 512), (48, 384), (48, 384), (48, 512))
BACK_CUT = (384, 768, 256, 128, 128, 256)


def work_shapes(rows, lanes, cut):
    held = lambda *dims: pltpu.VMEM((*dims, rows, lanes), jnp.bfloat16)
    part = lambda size: pltpu.VMEM((4, rows, size), jnp.bfloat16)
    return [held(4, 2, 2), held(4, 2, 2), part(cut), part(lanes - cut), held(4), held(4), held(3)]


def attend_back(proj, grads_in, probs, grads, vectors, row, length, group):
    rows = pl.ds(row, length)
    lane = lax.broadcasted_iota(jnp.int32, (length, 128), 1)
    score_scale = 1.0 / math.sqrt(HD)
    width = padded(length)

    def pair(p):
        at = lambda base: pl.ds(base + p * 128, 128)
        query, key, value = (proj[:length, at(base)] for base in (0, 256, 512))
        context_grad = grads_in[:length, at(0)]
        low = probs[p, :length, : 2 * width]
        weight = low.astype(jnp.float32)
        weight_grad = dot(context_grad, two_heads(value, width), NT)
        parts = []
        for h in (0, 1):
            lanes = slice(width * h, width * h + width)
            inner = jnp.sum(weight_grad[:, lanes] * weight[:, lanes], axis=1, keepdims=True)
            parts.append((weight[:, lanes] * (weight_grad[:, lanes] - inner)).astype(jnp.bfloat16))
        score_grad = jnp.concatenate(parts, axis=1)
        query_grad = dot(score_grad, two_heads(key, width), NN)
        key_grads = dot(score_grad, query, TN)
        value_grads = dot(low, context_grad, TN)
        both = lambda grad: jnp.where(lane < 64, grad[:length], grad[width : width + length])
        query_low = (query_grad * score_scale).astype(jnp.bfloat16)
        key_low = (both(key_grads) * score_scale).astype(jnp.bfloat16)
        value_low = both(value_grads).astype(jnp.bfloat16)
        grads[rows, at(768 * group)] = query_low
        grads[rows, at(768 * group + 256)] = key_low
        grads[rows, at(768 * group + 512)] = value_low
        vectors[0:1, at(256 * group)] += jnp.sum(query_low.astype(jnp.float32), axis=0, keepdims=True)
        vectors[1:2, at(256 * group)] += jnp.sum(value_low.astype(jnp.float32), axis=0, keepdims=True)

    for p in range(2):
        pair(p)


def vectors_on_wire(vectors, out, low):
    lane = lax.broadcasted_iota(jnp.int32, (512, 768), 1)
    start = (lax.broadcasted_iota(jnp.int32, (512, 768), 0) >> 4) * 24
    wide = jnp.broadcast_to(vectors[:, :768][None], (32, 16, 768)).reshape(512, 768)
    wide = jnp.where((lane >= start) & (lane < start + 24), wide, 0.0).astype(jnp.bfloat16)
    rows = dot(wide, spread_table(24, 768), NT).reshape(32, 16, 128)
    lane = lax.broadcasted_iota(jnp.int32, (32, 3072), 1)
    start = lax.broadcasted_iota(jnp.int32, (32, 3072), 0) * 96
    wide = jnp.where((lane >= start) & (lane < start + 96), vectors[9:10, :], 0.0).astype(jnp.bfloat16)
    up_rows = dot(wide, spread_table(96, 3072), NT)
    number = lax.broadcasted_iota(jnp.int32, (32, 16, 128), 1)
    rows = jnp.where(number == 5, up_rows[:, None, :], rows).astype(jnp.bfloat16)
    for i in range(32):
        out[i // 8, (i // 4) % 2, (i // 2) % 2, i % 2, :16, low : low + 128] = rows[i]
        out[i // 8, (i // 4) % 2, (i // 2) % 2, i % 2, 16:, low : low + 128] = jnp.zeros((32, 128), jnp.bfloat16)


def wire_blocks(total, out, left=0, right=384, lanes=384, low=0):
    for i in range(32):
        rows = slice(24 * i, 24 * i + 24)
        both = jnp.concatenate([total[rows, left : left + lanes], total[rows, right : right + lanes]], axis=0)
        out[i // 8, (i // 4) % 2, (i // 2) % 2, i % 2, :, low : low + lanes] = both.astype(jnp.bfloat16)


def last_kernel(*refs):
    act, pre, hidden, ffn, attn, final, embed_grad, context, proj, context_grad, ps, pls, w_qkv_in = refs[:13]
    sums, x_in = refs[13:15]
    part_out, d_out, u_out, o_out, g0_out, g1_out, g2_out, p_down, p_up = refs[15:24]
    stage, p_out, p_first, p_second, p_third, slot_proj, slot_grad, slot_pl, grads, w_qkv, total, vectors, token_part, eg_held, x_ref = refs[24:39]
    work, (send, recv, local, load, fetch, away) = refs[39 : 39 + 7 * len(BACK)], refs[39 + 7 * len(BACK) :]
    groups = (p_first, p_second, p_third)
    mine = (p_down, p_up, p_out, *groups)
    down, up, out, *heads = pieces = [
        Scatter(one, BACK_CUT[i], work[7 * i : 7 * i + 7], send, recv, local, i) for i, one in enumerate(mine)
    ]
    merges, bends, closes = ([[functools.partial(getattr(one, name), d) for d in range(4)] for one in pieces] for name in ("merge", "bend", "close"))
    bends, closes = ([[rows[d] for d in (1, 2, 3, 0)] for rows in kind] for kind in (bends, closes))
    stores = (d_out, u_out, o_out, g0_out, g1_out, g2_out)
    ends = [functools.partial(one.result, store) for one, store in zip(pieces, stores)]

    s0, s1, s2, s3 = [grads.at[:, pl.ds(768 * i, 768)] for i in range(3)] + [token_part]
    halves = lambda j, slot: [
        (pre.at[:, pl.ds(384 * j, 384)], slot.at[:, pl.ds(0, 384)]),
        (pre.at[:, pl.ds(1536 + 384 * j, 384)], slot.at[:, pl.ds(384, 384)]),
    ]
    acts = lambda j, slot: [(act.at[:, pl.ds(768 * j, 768)], slot)]
    started, carried = [], []

    def bring(pairs):
        copies = []
        for source, target in pairs:
            copies.append(pltpu.make_async_copy(source, target, fetch.at[len(started)]))
            copies[-1].start()
            started.append(copies[-1])
        return copies

    def have(copies):
        for copy in copies:
            copy.wait()

    def carry(source, target):
        copy = pltpu.make_async_copy(source, target, away.at[len(carried)])
        copy.start()
        carried.append(copy)
        return copy

    ffn_here, here = bring([(ffn, s0)]), {}
    for j, slot in enumerate((s1, s2, s3)):
        here["act", j] = bring(acts(j, slot))
    eg_here = bring([(embed_grad, eg_held)])
    lanes = [(w_qkv_in.at[:, pl.ds(768 * p + 256 * g, 256)], w_qkv.at[:, pl.ds(768 * g + 256 * p, 256)]) for g in range(3) for p in range(3)]
    vectors[...] = sums[...]
    greet(*place())
    have(ffn_here)
    sent = {}
    for j, slot in enumerate((s1, s2, s3, s1)):
        have(here["act", j])
        low = dot(slot[...], s0[...], TN).astype(jnp.bfloat16)
        if j >= 2:
            sent[j - 2].wait()
        stage[j % 2] = low.reshape(2, 2, 2, 96, 768)
        sent[j] = carry(stage.at[j % 2], p_down.at[j])
        if j == 0:
            here["act", 3] = bring(acts(3, s1))
        elif j == 1:
            hidden_here = bring([(hidden, s2)])
        elif j == 2:
            here["pre", 0] = bring(halves(0, s3))
    here["pre", 1] = bring(halves(1, s0))
    here["pre", 2] = bring(halves(2, s1))
    have(hidden_here)
    hooks = iter([[], merges[0][:1], merges[0][1:], bends[0][:1]])
    for j, slot in enumerate((s3, s0, s1, s3)):
        have(here["pre", j])
        total[...] = dot(s2[...], slot[...], TN)
        if j == 0:
            sent[2].wait()
            sent[3].wait()
            down.start()
        held = groups[j % 2]
        if j >= 2:
            sent[j + 2].wait()
        wire_blocks(total, held)
        sent[4 + j] = carry(held.at[:, :, :, :, :, pl.ds(0, 384)], p_up.at[:, :, :, :, :, pl.ds(384 * j, 384)])
        if j == 0:
            here["pre", 3] = bring(halves(3, s3))
        elif j == 1:
            context_here = bring([(context, s0)])
        elif j == 2:
            attn_here = bring([(attn, s1)])
        for step in next(hooks):
            step()
    final_here = bring([(final, s2)])
    x_here = bring([(x_in, x_ref)])
    weights_here = bring(lanes)
    order = [(SHORT + 320 * s, 320, s) for s in range(4)] + [(128 * s, 128, s) for s in range(4)]
    order = [(g, *one) for g in range(3) for one in order]

    def loads(n):
        group, row, length, s = order[n]
        slot = n % 2
        rows = pl.ds(row, length)
        copies = [
            (proj.at[rows, pl.ds(768 * p + 256 * group, 256)], slot_proj.at[slot, pl.ds(0, length), pl.ds(256 * p, 256)]) for p in range(3)
        ]
        copies.append((context_grad.at[rows, pl.ds(256 * group, 256)], slot_grad.at[slot, pl.ds(0, length)]))
        source = pls if length == 320 else ps
        copies.append((source.at[s, pl.ds(2 * group, 2)], slot_pl.at[slot, :, pl.ds(0, length), pl.ds(0, 2 * padded(length))]))
        return [pltpu.make_async_copy(source, target, load.at[slot, i]) for i, (source, target) in enumerate(copies)]

    for copy in loads(0):
        copy.start()
    have(context_here)
    have(attn_here)
    total[...] = dot(s0[...], s1[...], TN)
    sent[6].wait()
    sent[7].wait()
    up.start()
    wire_blocks(total, p_out)
    for step in bends[0][1:3]:
        step()
    have(final_here)
    have(eg_here)
    total[:, :128] = dot(s2[...], eg_held[...], TN)
    wire_blocks(total, p_out, 0, 0, 128, 384)
    out.start()
    hooks = iter([
        [*bends[0][3:], merges[1][0]], merges[1][1:], [merges[2][0]], merges[2][1:], [], [], closes[0][:2], closes[0][2:], [],
        [merges[3][0], *bends[1][:1]], [*merges[3][1:], *bends[1][1:2]], bends[1][2:3], bends[1][3:], bends[2][:2], bends[2][2:], bends[3][:2], bends[3][2:], [],
        [merges[4][0], *closes[1][:1]], [*merges[4][1:], *closes[1][1:2]], closes[1][2:3], closes[1][3:], closes[2][:2], closes[2][2:], bends[4][:2], bends[4][2:], [ends[0]],
        [merges[5][0], *closes[3][:2]], [*merges[5][1:], *closes[3][2:]], closes[4][:2], [*closes[4][2:], *bends[5][:2]], bends[5][2:],
    ])

    def hook():
        for step in next(hooks):
            step()

    for n, (group, row, length, s) in enumerate(order):
        if n + 1 < len(order):
            for copy in loads(n + 1):
                copy.start()
        for copy in loads(n):
            copy.wait()
        slot = n % 2
        attend_back(slot_proj.at[slot], slot_grad.at[slot], slot_pl.at[slot], grads, vectors, row, length, group)
        hook()
        if n % 8 == 7:
            if group == 0:
                have(x_here)
            total[...] = dot(x_ref[...], grads[:, 768 * group : 768 * group + 768], TN)
            if group == 2:
                vectors_on_wire(vectors, p_third, 384)
            wire_blocks(total, groups[group])
            heads[group].start()
            hook()
    have(weights_here)
    for row, length in [(0, SHORT)] + [(SHORT + 320 * s, 320) for s in range(4)]:
        rows = pl.ds(row, length)
        token_part[rows] = dot(grads[rows], w_qkv[...], NT).astype(jnp.bfloat16)
        carry(token_part.at[rows], part_out.at[rows])
        hook()
    for step in [ends[1], *closes[5], ends[2], ends[3], ends[4], ends[5]]:
        step()
    for copy in carried[8:]:
        copy.wait()
    for piece in pieces:
        piece.drain()


def last(operands, sums, x):
    vmem, anywhere = (pl.BlockSpec(memory_space=m) for m in (pltpu.VMEM, pl.ANY))
    full = lambda *dims: jax.ShapeDtypeStruct(dims, jnp.float32)
    low = lambda *dims: jax.ShapeDtypeStruct(dims, jnp.bfloat16)
    held = lambda *dims: pltpu.VMEM(dims, jnp.bfloat16)
    semaphores = lambda *dims: pltpu.SemaphoreType.DMA(dims)
    scratch = []
    for dims, cut in zip(BACK, BACK_CUT):
        scratch += work_shapes(*dims, cut)
    return pl.pallas_call(
        last_kernel,
        out_shape=(low(ROWS, 768), *[full(*dims) for dims in BACK], *[low(4, 2, 2, 2, *dims) for dims in BACK[:2]]),
        in_specs=[anywhere] * 13 + [vmem, anywhere],
        out_specs=(anywhere,) + (vmem,) * 6 + (anywhere,) * 2,
        scratch_shapes=[held(2, 2, 2, 2, 96, 768)]
        + [held(4, 2, 2, 2, *dims) for dims in BACK[2:]]
        + [held(2, 320, 768), held(2, 320, 256), held(2, 2, 320, 768), held(ROWS, 2304), held(768, 2304)]
        + [pltpu.VMEM((768, 768), jnp.float32), pltpu.VMEM((16, 3072), jnp.float32), held(ROWS, 768), held(ROWS, P_SIZE), held(ROWS, 768)]
        + scratch
        + [semaphores(SUMS * len(BACK)), semaphores(SUMS * len(BACK)), semaphores(len(BACK)), semaphores(2, 5), semaphores(32), semaphores(16)],
        compiler_params=pltpu.CompilerParams(collective_id=1, has_side_effects=True, vmem_limit_bytes=63 * 2**20),
    )(*operands, sums, x)[:7]


def finish_kernel(resid, part, d, u, o, g0, g1, g2, gs, gl, q_out, k_out, v_out, o_out, u_out, d_out, e_out, *vectors):
    tile = pl.program_id(0)
    value = resid[...] + part[...].astype(jnp.float32)

    @pl.when(tile < 2)
    def _():
        gs[...] = value

    @pl.when(tile >= 2)
    def _():
        gl[...] = value

    @pl.when(tile == 0)
    def _():
        d_out[...] = d[...]
        for wire, target, half in ((u, u_out, 1536), (o, o_out, 384)):
            target[:, :half] = wire[:24, :half]
            target[:, half:] = wire[24:, :half]
        e_out[...] = o[:24, 384:]
        for g, wire in enumerate((g0, g1, g2)):
            low = 256 * g
            q_out[:, low : low + 256] = wire[:24, :256]
            k_out[:, low : low + 128] = wire[:24, 256:384]
            k_out[:, low + 128 : low + 256] = wire[24:, :128]
            v_out[:, low : low + 256] = wire[24:, 128:384]
        for i, target in enumerate(vectors):
            width = target.shape[0]
            target[...] = g2[i : i + 1, 384 : 384 + width].reshape(width)


def finish(resid, part, wires, shards):
    tile = 256
    full = lambda *dims: jax.ShapeDtypeStruct(dims, jnp.float32)
    every = pl.BlockSpec((tile, 768), lambda i: (i, 0))
    whole = lambda one: pl.BlockSpec(one.shape, lambda i: (0,) * one.ndim)
    cut = SHORT // tile
    query, key, value, out, up, down, embed, *vectors = shards
    return pl.pallas_call(
        finish_kernel,
        grid=(ROWS // tile,),
        out_shape=(full(SHORT, 768), full(ROWS - SHORT, 768), *[full(*one.shape) for one in shards]),
        in_specs=[every, every] + [whole(one) for one in wires],
        out_specs=(
            pl.BlockSpec((tile, 768), lambda i: (jnp.minimum(i, cut - 1), 0)),
            pl.BlockSpec((tile, 768), lambda i: (jnp.maximum(i - cut, 0), 0)),
            *[whole(one) for one in shards],
        ),
        compiler_params=pltpu.CompilerParams(vmem_limit_bytes=62 * 2**20),
    )(resid, part, *wires)


def fast_body(xs, len_short, xl, len_long, shards, cs, cl):
    flat = lambda one: one.reshape(-1, one.shape[-1])
    w_qkv, w_out, w_up, w_embed, w_down, vec, proj, context, ps, pls, x, cot = first(
        len_short, len_long, flat(xs), flat(xl), flat(cs), flat(cl), shards
    )
    es, el, act, pre, hidden, ffn, attn, final, embed_grad, resid, context_grad, sums = token_chain(
        len_short, len_long, x, cot, context, w_out, w_up, w_down.reshape(3072, 768), w_embed, vec
    )
    part, *wires = last((act, pre, hidden, ffn, attn, final, embed_grad, context, proj, context_grad, ps, pls, w_qkv), sums, x)
    gs, gl, *owned = finish(resid, part, wires, shards)
    shaped = lambda value, like: value.reshape(*like.shape[:2], -1)
    return (shaped(es, xs), shaped(el, xl), shaped(gs, xs), shaped(gl, xl), *owned)


def body(tokens_short, lengths_short, tokens_long, lengths_long, *rest):
    shards, (cotangent_short, cotangent_long) = rest[:16], rest[16:]
    weights = tuple(lax.all_gather(one, BOTH, axis=0, tiled=True) for one in shards)
    embed_short, saved_short = forward(tokens_short, lengths_short, weights)
    embed_long, saved_long = forward(tokens_long, lengths_long, weights)
    input_short, grads_short = backward(saved_short, weights, cotangent_short)
    input_long, grads_long = backward(saved_long, weights, cotangent_long)
    totals = jax.tree.map(jnp.add, grads_short, grads_long)
    owned = tuple(lax.psum_scatter(one, BOTH, scatter_dimension=0, tiled=True) for one in totals)
    return (embed_short, embed_long, input_short, input_long, *owned)


def solution(mesh):
    split = lambda rank: P(BOTH, *([None] * (rank - 1)))
    weights = [split(2)] * 7 + [split(1)] * 9
    in_specs = (split(3), split(1), split(3), split(1), *weights, split(3), split(3))
    out_specs = (split(3),) * 4 + tuple(weights)
    fast = mesh.shape["wide"] == 16 and mesh.shape["narrow"] == 2

    def step(xs, len_short, xl, len_long, *rest):
        if fast:
            return fast_body(xs, len_short, xl, len_long, rest[:16], *rest[16:])
        return body(xs, len_short, xl, len_long, *rest)

    return jax.shard_map(step, mesh=mesh, in_specs=in_specs, out_specs=out_specs, check_vma=False)
```

profile of v0, /device:TPU:0, one launch (start us, length us, event | category | flops | bytes accessed | tf_op | source)
XLA Modules:
  0.0 257.8 jit_solution(7598414148875009612)
XLA Ops:
  0.7 81.7 %shard_map.365 = (bf16[768,2304]{1,0:T(8,128)(2,1)}, bf16[768,768]{1,0:T(8,128)(2,1)}, bf16[768,3072]{1,0:T(8,128)(2,1)}, bf16[768,128]{1,0:T(8,128)(2,1)}, bf16...) custom-call(s32[4]{0:T(128)} %len_short.3, ...), custom_call_target="tpu_custom_call" | custom-call | tf_op jit(solution)/shard_map/pallas_call | solution.py:564
  82.3 61.4 %shard_map.366 = (f32[512,128]{1,0:T(8,128)}, f32[1280,128]{1,0:T(8,128)}, bf16[1792,3072]{1,0:T(8,128)(2,1)}, bf16[1792,3072]{1,0:T(8,128)(2,1)}, bf16[1792,768...) custom-call(s32[4]{0:T(128)} %len_short.3, ...), custom_call_target="tpu_custom_call" | custom-call | tf_op jit(solution)/shard_map/pallas_call | solution.py:712
  143.8 104.9 %shard_map.367 = (bf16[1792,768]{1,0:T(8,128)(2,1)}, f32[96,768]{1,0:T(8,128)}, f32[48,1536]{1,0:T(8,128)}, f32[48,512]{1,0:T(8,128)}, f32[48,384]{1,0:T(8,128)}...) custom-call(bf16[1792,3072]{1,0:T(8,128)(2,1)} %get-tuple-element.80, ...), custom_call_target="tpu_custom_call" | custom-call | tf_op jit(solution)/shard_map/pallas_call | solution.py:1083
  248.7 8.6 %shard_map.368 = (f32[512,768]{1,0:T(8,128)}, f32[1280,768]{1,0:T(8,128)}, f32[24,768]{1,0:T(8,128)}, f32[24,768]{1,0:T(8,128)}, f32[24,768]{1,0:T(8,128)}, /*in...) custom-call(f32[1792,768]{1,0:T(8,128)} %get-tuple-element.79.resid,, ...), custom_call_target="tpu_custom_call" | custom-call | tf_op jit(solution)/shard_map/pallas_call | solution.py:1135
where the time goes:
time: 262 us; the launch traced here: 258 us
  Pallas kernels  257 us (98%)
    pallas_call x1, Pallas kernels, last(): pl.pallas_call(last_kernel, out_shape=(low(ROWS, 768), *[full(*dims) for...  105 us
    pallas_call x1, Pallas kernels, first(): pl.pallas_call(first_kernel, out_shape=(*[low(*dims) for dims in weights]...  81.7 us
    pallas_call x1, Pallas kernels, token_chain(): pl.pallas_call(token_kernel, grid=(ROWS // TILE,), out_shape=(shape(jnp.f...  61.4 us
    pallas_call x1, Pallas kernels, finish(): pl.pallas_call(finish_kernel, grid=(ROWS // tile,), out_shape=(full(SHORT...  8.59 us

commit v1 on v0

--- a/solution.py
+++ b/solution.py
@@ -1030,9 +1030,9 @@
     out.start()
     hooks = iter([
         [*bends[0][3:], merges[1][0]], merges[1][1:], [merges[2][0]], merges[2][1:], [], [], closes[0][:2], closes[0][2:], [],
-        [merges[3][0], *bends[1][:1]], [*merges[3][1:], *bends[1][1:2]], bends[1][2:3], bends[1][3:], bends[2][:2], bends[2][2:], bends[3][:2], bends[3][2:], [],
-        [merges[4][0], *closes[1][:1]], [*merges[4][1:], *closes[1][1:2]], closes[1][2:3], closes[1][3:], closes[2][:2], closes[2][2:], bends[4][:2], bends[4][2:], [ends[0]],
-        [merges[5][0], *closes[3][:2]], [*merges[5][1:], *closes[3][2:]], closes[4][:2], [*closes[4][2:], *bends[5][:2]], bends[5][2:],
+        bends[1][:1], [merges[3][0], *bends[1][1:2]], [*merges[3][1:], *bends[1][2:3]], bends[1][3:], bends[2][:2], bends[2][2:], [], bends[3][:2], bends[3][2:],
+        closes[1][:1], [merges[4][0], *closes[1][1:2]], [*merges[4][1:], *closes[1][2:3]], closes[1][3:], closes[2][:2], closes[2][2:], bends[4][:2], bends[4][2:], [ends[0]],
+        [*closes[3][:2], merges[5][0]], [*merges[5][1:], *closes[3][2:]], closes[4][:2], [*closes[4][2:], *bends[5][:2]], bends[5][2:],
     ])
 
     def hook():

time: 262 us -> 261 us (level)
  no operation moved by 1% of the time
where the time goes in v1:
time: 261 us; the launch traced here: 258 us
  Pallas kernels  256 us (98%)
    pallas_call x1, Pallas kernels, last(): pl.pallas_call(last_kernel, out_shape=(low(ROWS, 768), *[full(*dims) for...  105 us
    pallas_call x1, Pallas kernels, first(): pl.pallas_call(first_kernel, out_shape=(*[low(*dims) for dims in weights]...  81.7 us
    pallas_call x1, Pallas kernels, token_chain(): pl.pallas_call(token_kernel, grid=(ROWS // TILE,), out_shape=(shape(jnp.f...  61.4 us
    pallas_call x1, Pallas kernels, finish(): pl.pallas_call(finish_kernel, grid=(ROWS // tile,), out_shape=(full(SHORT...  8.59 us

profile of v1, /device:TPU:0, one launch (start us, length us, event | category | flops | bytes accessed | tf_op | source)
XLA Modules:
  0.0 257.6 jit_solution(1869455149736119495)
XLA Ops:
  0.7 81.7 %shard_map.365 = (bf16[768,2304]{1,0:T(8,128)(2,1)}, bf16[768,768]{1,0:T(8,128)(2,1)}, bf16[768,3072]{1,0:T(8,128)(2,1)}, bf16[768,128]{1,0:T(8,128)(2,1)}, bf16...) custom-call(s32[4]{0:T(128)} %len_short.3, ...), custom_call_target="tpu_custom_call" | custom-call | tf_op jit(solution)/shard_map/pallas_call | solution.py:564
  82.3 61.4 %shard_map.366 = (f32[512,128]{1,0:T(8,128)}, f32[1280,128]{1,0:T(8,128)}, bf16[1792,3072]{1,0:T(8,128)(2,1)}, bf16[1792,3072]{1,0:T(8,128)(2,1)}, bf16[1792,768...) custom-call(s32[4]{0:T(128)} %len_short.3, ...), custom_call_target="tpu_custom_call" | custom-call | tf_op jit(solution)/shard_map/pallas_call | solution.py:712
  143.8 104.7 %shard_map.367 = (bf16[1792,768]{1,0:T(8,128)(2,1)}, f32[96,768]{1,0:T(8,128)}, f32[48,1536]{1,0:T(8,128)}, f32[48,512]{1,0:T(8,128)}, f32[48,384]{1,0:T(8,128)}...) custom-call(bf16[1792,3072]{1,0:T(8,128)(2,1)} %get-tuple-element.80, ...), custom_call_target="tpu_custom_call" | custom-call | tf_op jit(solution)/shard_map/pallas_call | solution.py:1083
  248.5 8.6 %shard_map.368 = (f32[512,768]{1,0:T(8,128)}, f32[1280,768]{1,0:T(8,128)}, f32[24,768]{1,0:T(8,128)}, f32[24,768]{1,0:T(8,128)}, f32[24,768]{1,0:T(8,128)}, /*in...) custom-call(f32[1792,768]{1,0:T(8,128)} %get-tuple-element.79.resid,, ...), custom_call_target="tpu_custom_call" | custom-call | tf_op jit(solution)/shard_map/pallas_call | solution.py:1135
